TPU v7x, 128 devices: a whole 4x4x4 slice. The times are simulated.
128 devices in a mesh: group: 4 (over x_lo, core), tensor: 32 (over x_hi, y, z).
Axes of the slice: x: 4 (x_hi: 2, x_lo: 2; x = x_hi * 2 + x_lo), y: 4, z: 4, core: 2. Of those that a mesh axis runs over, the one named last changes fastest.
Arguments:
- tokens: bfloat16 [512, 3, 8192], P(('group', 'tensor')), may hold values from -6 to 6
- norm_gain: float32 [8192], replicated, may hold values from 0.25 to 1.75
- w_qkv: bfloat16 [8192, 10240], P(None, 'tensor'), may hold values from -0.0625 to 0.0625
- w_out: bfloat16 [8192, 8192], P('tensor'), may hold values from -0.0625 to 0.0625
- lengths: int32 [128, 4], P(('group', 'tensor')), may hold values from 1 to 512, 1024 in all within a row
- migrate: int32 [128, 4], P(('group', 'tensor')), may hold values from 0 to 3, as said below
- page_order: int32 [128, 12], P(('group', 'tensor')), may hold values from 0 to 11, each once within a row
- kv_pool: bfloat16 [128, 12, 2, 8, 128, 128], P(('group', 'tensor')), as said below
Outputs:
- mixed: bfloat16 [512, 3, 8192], P(('group', 'tensor'))
Inputs may be any that keep to these rules, and one draw needn't show every extreme that they name: `migrate`: on each device every group number is named by exactly 1 row. The 4 lengths of one device sum to 1024. `kv_pool`: cached keys and values of order one or more.
All inputs are finite; a program needn't handle non-finite values.
Results may differ from a plain program's by a relative error of at most 0.013.
Values may be sent and summed in bfloat16 or wider, within the bound.
A program may use at most 128 MiB of HBM per device.

v0:
```python
import jax
import jax.numpy as jnp
from jax import lax
from jax.sharding import Mesh
from jax.sharding import PartitionSpec as P

HEADS = 64
KV_HEADS = 8
HEAD_DIM = 128
PAGE = 128
MAX_PAGES = 4
GROUP = ("group_0", "group_1")
GROUP_TENSOR = ("group_0", "group_1", "tensor")
EPS = 1e-05
ROPE_BASE = 500000.0
NEG_FILL = -1e30


def cut_along(shard, dim, devices):
    lengths = shard.shape
    parts = shard.reshape(*lengths[:dim], devices, lengths[dim] // devices, *lengths[dim + 1 :])
    return jnp.moveaxis(parts, dim, 0)


def joined_along(parts, dim):
    parts = jnp.moveaxis(parts, 0, dim)
    lengths = parts.shape
    return parts.reshape(*lengths[:dim], lengths[dim] * lengths[dim + 1], *lengths[dim + 2 :])


def moved_by_axis(parts, axes, sequence):
    inside = parts.shape[1:]
    out = parts.reshape(*(lax.axis_size(a) for a in axes), *inside)
    for k in sequence:
        out = lax.all_to_all(out, axes[k], k, k, tiled=True)
    return out.reshape(-1, *inside)


def stepwise_exchange(shard, axes, sequence, split_dim, concat_dim):
    parts = cut_along(shard, split_dim, lax.axis_size(axes))
    return joined_along(moved_by_axis(parts, axes, sequence), concat_dim)


def side_by_side(arrays, axis, split_dim, concat_dim, along):
    columns = [a.reshape(*a.shape[:along], -1) for a in arrays]
    both = jnp.concatenate(columns, axis=along)
    out, at, gathered = (
        lax.all_to_all(both, axis, split_axis=split_dim, concat_axis=concat_dim, tiled=True),
        0,
        [],
    )
    for a, column in zip(arrays, columns):
        piece = out[..., at : at + column.shape[along]]
        gathered.append(piece.reshape(*piece.shape[:along], *a.shape[along:]))
        at += column.shape[along]
    return tuple(gathered)


def summed_on_arrival(shard, axis, dim):
    parts = cut_along(shard, dim, lax.axis_size(axis))
    arrived = lax.all_to_all(parts, axis, split_axis=0, concat_axis=0, tiled=True)
    return arrived.astype(jnp.float32).sum(axis=0)


def rotate(values, positions):
    half_dim = values.shape[-1] // 2
    inverse = ROPE_BASE ** (-(jnp.arange(half_dim, dtype=jnp.float32) * 2.0 / values.shape[-1]))
    angles = positions.astype(jnp.float32)[..., None] * inverse
    cosine = jnp.cos(angles)[..., None, :]
    sine = jnp.sin(angles)[..., None, :]
    lower_half = values[..., :half_dim]
    upper_half = values[..., half_dim:]
    return jnp.concatenate(
        [lower_half * cosine - upper_half * sine, upper_half * cosine + lower_half * sine], axis=-1
    )


def cache_stats(queries, pages, row_lens):
    row_total, steps_here, head_count, head_dim = queries.shape
    page_count = pages.shape[1]
    kv_heads = pages.shape[3]
    page_len = pages.shape[4]
    grouped = queries.reshape(row_total, steps_here, kv_heads, head_count // kv_heads, head_dim)
    scores = jnp.einsum(
        "rskgd,rbktd->rskgbt", grouped, pages[:, :, 0], preferred_element_type=jnp.float32
    ) * head_dim ** (-0.5)
    places = (
        jnp.arange(page_count, dtype=jnp.int32)[:, None] * page_len
        + jnp.arange(page_len, dtype=jnp.int32)[None, :]
    )
    inside = (places[None] < row_lens[:, None, None])[:, None, None, None]
    page_top = jnp.max(jnp.where(inside, scores, NEG_FILL), axis=-1)
    weights = jnp.where(inside, jnp.exp(scores - page_top[..., None]), 0.0).astype(jnp.bfloat16)
    page_total = jnp.sum(weights.astype(jnp.float32), axis=-1)
    page_acc = jnp.einsum(
        "rskgbt,rbktd->rskgbd", weights, pages[:, :, 1], preferred_element_type=jnp.float32
    )
    top_score = jnp.max(page_top, axis=-1)
    page_scale = jnp.exp(page_top - top_score[..., None])
    return (
        top_score,
        jnp.sum(page_scale * page_total, axis=-1),
        jnp.sum(page_scale[..., None] * page_acc, axis=-2),
    )


def finish(queries, cache_parts, all_keys, all_values):
    row_total, steps_here, head_count, head_dim = queries.shape
    kv_heads = all_keys.shape[2]
    grouped = queries.reshape(row_total, steps_here, kv_heads, head_count // kv_heads, head_dim)
    scores = jnp.einsum(
        "rskgd,rukd->rskgu", grouped, all_keys, preferred_element_type=jnp.float32
    ) * head_dim ** (-0.5)
    allowed = jnp.arange(all_keys.shape[1])[None, :] <= jnp.arange(steps_here)[:, None]
    allowed = allowed[None, :, None, None, :]
    new_top = jnp.max(jnp.where(allowed, scores, NEG_FILL), axis=-1)
    weights = jnp.where(allowed, jnp.exp(scores - new_top[..., None]), 0.0).astype(jnp.bfloat16)
    new_total = jnp.sum(weights.astype(jnp.float32), axis=-1)
    new_acc = jnp.einsum(
        "rskgu,rukd->rskgd", weights, all_values, preferred_element_type=jnp.float32
    )
    cache_top, cache_total, cache_acc = cache_parts
    top_score = jnp.maximum(cache_top, new_top)
    cache_scale = jnp.exp(cache_top - top_score)
    new_scale = jnp.exp(new_top - top_score)
    merged = (cache_scale[..., None] * cache_acc + new_scale[..., None] * new_acc) / (
        cache_scale * cache_total + new_scale * new_total
    )[..., None]
    return merged.reshape(row_total, steps_here, head_count * head_dim).astype(jnp.bfloat16)


def per_device(tokens, norm_gain, w_qkv, w_out, lengths, migrate, page_order, kv_pool):
    row_lens = lengths[0]
    destinations = migrate[0]
    pool_order = page_order[0]
    page_pool = kv_pool[0]
    row_total = row_lens.shape[0]
    pool_size = page_pool.shape[0]
    slot_ids = jnp.arange(row_total, dtype=jnp.int32)
    sort_keys = destinations * row_total + slot_ids
    row_ranks = jnp.sum((sort_keys[None, :] < sort_keys[:, None]).astype(jnp.int32), axis=1)
    placing = row_ranks[:, None] == slot_ids[None, :]
    pages_used = (row_lens + PAGE - 1) // PAGE
    offsets = jnp.cumsum(pages_used) - pages_used
    sorted_lens = jnp.sum(jnp.where(placing, row_lens[:, None], 0), axis=0)
    sorted_first = jnp.sum(jnp.where(placing, offsets[:, None], 0), axis=0)
    page_slots = jnp.clip(
        sorted_first[:, None] + jnp.arange(MAX_PAGES, dtype=jnp.int32)[None, :], 0, pool_size - 1
    )
    home_pages = page_pool[pool_order[page_slots]]
    new_lens = stepwise_exchange(sorted_lens, GROUP, (0, 1), 0, 0)
    width_q = HEADS * HEAD_DIM
    width_k = KV_HEADS * HEAD_DIM
    keys_so_far = jnp.zeros((row_total, 0, KV_HEADS, HEAD_DIM), jnp.bfloat16)
    values_so_far = jnp.zeros((row_total, 0, KV_HEADS, HEAD_DIM), jnp.bfloat16)
    steps_here = tokens.shape[1]
    floats = tokens.astype(jnp.float32)
    normed = (
        floats * lax.rsqrt(jnp.mean(floats * floats, axis=-1, keepdims=True) + EPS) * norm_gain
    ).astype(jnp.bfloat16)

    def columns(row_piece, row_start):
        return jnp.einsum(
            "rsd,dc->rsc", row_piece, w_qkv, preferred_element_type=jnp.float32
        ).astype(jnp.bfloat16)

    gathered = columns(lax.all_gather(normed, "tensor", axis=0, tiled=True), jnp.int32(0))
    full_rows = lax.all_to_all(gathered, "tensor", split_axis=0, concat_axis=2, tiled=True)
    positions = new_lens[:, None] + 0 + jnp.arange(steps_here, dtype=jnp.int32)[None, :]
    queries = rotate(
        full_rows[..., :width_q]
        .reshape(row_total, steps_here, HEADS, HEAD_DIM)
        .astype(jnp.float32),
        positions,
    ).astype(jnp.bfloat16)
    keys_here = rotate(
        full_rows[..., width_q : width_q + width_k]
        .reshape(row_total, steps_here, KV_HEADS, HEAD_DIM)
        .astype(jnp.float32),
        positions,
    ).astype(jnp.bfloat16)
    values_here = full_rows[..., width_q + width_k :].reshape(
        row_total, steps_here, KV_HEADS, HEAD_DIM
    )
    all_keys = jnp.concatenate([keys_so_far, keys_here], axis=1)
    all_values = jnp.concatenate([values_so_far, values_here], axis=1)
    home_queries = lax.all_to_all(queries, GROUP, split_axis=0, concat_axis=0, tiled=True)
    home_parts = cache_stats(home_queries, home_pages, sorted_lens)
    attended = finish(
        queries,
        tuple(
            (
                part.astype(jnp.float32)
                for part in side_by_side(
                    (
                        home_parts[0].astype(jnp.bfloat16),
                        home_parts[1].astype(jnp.bfloat16),
                        home_parts[2].astype(jnp.bfloat16),
                    ),
                    GROUP,
                    0,
                    0,
                    4,
                )
            )
        ),
        all_keys,
        all_values,
    )
    spread = lax.all_to_all(attended, "tensor", split_axis=2, concat_axis=0, tiled=True)
    summed = summed_on_arrival(
        jnp.einsum("rsc,cd->rsd", spread, w_out, preferred_element_type=jnp.float32).astype(
            jnp.bfloat16
        ),
        "tensor",
        0,
    )
    output = (floats + summed).astype(jnp.bfloat16)
    return output


def solution(mesh):
    split = Mesh(mesh.devices.reshape(2, 2, mesh.shape["tensor"]), ("group_0", "group_1", "tensor"))
    placed = (
        P(GROUP_TENSOR, None, None),
        P(),
        P(None, "tensor"),
        P("tensor", None),
        P(GROUP_TENSOR, None),
        P(GROUP_TENSOR, None),
        P(GROUP_TENSOR, None),
        P(GROUP_TENSOR, None, None, None, None, None),
    )
    return jax.shard_map(
        per_device,
        mesh=split,
        in_specs=placed,
        out_specs=P(GROUP_TENSOR, None, None),
        check_vma=False,
    )
```

profile of v0, /device:TPU:0, one launch (start us, length us, event | category | flops | bytes accessed | tf_op | source)
XLA Modules:
  0.0 344.3 jit_solution(6098262649707031891)
XLA Ops:
  6.5 1.1 fusion.23
  7.7 1.1 fusion.25
  8.8 0.9 copy.227
  14.1 3.2 all-to-all-start.1
  18.3 7.7 %gather_fusion.1 = bf16[16,2,8,128,128]{4,3,2,1,0:T(8,128)(2,1)} fusion(bf16[12,2,8,128,128]{4,3,2,1,0:T(8,128)(2,1)} %bitcast.155, s32[1024]{0:T(1024)S(1)} %pad_clamp_fusion), kind=kCustom, calls=%fused_computation.1 | custom fusion | bytes 16777280 | tf_op jit(solution)/shard_map/gather | solution.py:150
  26.2 6.0 %fusion.46 = (bf16[4,4,1,8,128,128]{5,4,3,2,1,0:T(8,128)(2,1)}, bf16[4,4,1,8,128,128]{5,4,3,2,1,0:T(8,128)(2,1)}) fusion(bf16[4,4,2,8,128,128]{5,4,3,2,1,0:T(8,128)(2,1)} %bitcast.152), kind=kLoop, calls=%fused_computation.107 | loop fusion | bytes 16777216 | tf_op jit(solution)/shard_map/slice | solution.py:85
  32.3 3.6 %all_to_all.61 = s32[2,2,1]{0,2,1:T(1,128)S(1)} all-to-all(s32[2,2,1]{0,2,1:T(1,128)S(1)} %copy.233), channel_id=1, replica_groups=mesh['group_0'=2,'group_1'=2,'tensor'=32] {'group_1'}, dimensions={1} | all-to-all | bytes 32 | tf_op jit(solution)/shard_map/all_to_all | solution.py:35
  36.1 80.8 %all-gather.2.cloned.1.call-done = bf16[128,3,8192]{2,1,0:T(4,128)(2,1)} async-done(((bf16[4,3,8192]{2,1,0:T(4,128)(2,1)}), bf16[128,3,8192]{2,1,0:T(4,128)(2,1)}) %all-gather.2.cloned.1.call-update) | async-done | bytes 6291472 | tf_op jit(solution)/shard_map/all_gather | solution.py:167
  116.9 12.4 %fusion.16 = bf16[128,3,320]{0,2,1:T(8,128)(2,1)S(1)} fusion(bf16[8192,320]{0,1:T(8,128)(2,1)} %param.10, bf16[128,3,8192]{2,1,0:T(4,128)(2,1)} %all-gather.2.cloned.1.call-done), kind=kOutput, calls=%fused_computation.27 | convolution fusion | flops 2013388800 | bytes 11780096 | tf_op jit(solution)/shard_map/rsd,dc->rsc/dot_general | solution.py:163
  129.3 1.0 copy.229
  130.2 5.9 %all-to-all-start = ((bf16[128,3,320]{2,1,0:T(4,128)(2,1)}), bf16[128,3,320]{2,1,0:T(4,128)(2,1)S(1)}, u32[]{:S(2)}, u32[]{:S(2)}) async-start(bf16[128,3,320]{2,1,0:T(4,128)(2,1)} %copy.229), calls=%async_computation | async-start | bytes 786432 | tf_op jit(solution)/shard_map/all_to_all | solution.py:168
  136.4 11.0 %all-to-all-done = bf16[128,3,320]{2,1,0:T(4,128)(2,1)S(1)} async-done(((bf16[128,3,320]{2,1,0:T(4,128)(2,1)}), bf16[128,3,320]{2,1,0:T(4,128)(2,1)S(1)}, u32[]{:S(2)}, u32[]{:S(2)}) %all-to-all-start) | async-done | bytes 245792 | tf_op jit(solution)/shard_map/all_to_all | solution.py:168
  149.3 3.4 all-to-all-start.3
  152.7 5.2 %all-to-all-done.3 = bf16[4,3,64,128]{3,2,1,0:T(8,128)(2,1)S(1)} async-done(((bf16[4,3,64,128]{3,2,1,0:T(8,128)(2,1)}), bf16[4,3,64,128]{3,2,1,0:T(8,128)(2,1)S(1)}, u32[]{:S(2)}, u32[]{:S(2)}) %all-to-all-start.3) | async-done | bytes 196640 | tf_op jit(solution)/shard_map/all_to_all | solution.py:187
  158.0 3.6 %fusion.10 = (f32[4,3,8,8,4]{3,1,4,2,0:T(4,128)S(1)}, f32[4,8,4,128,3,8]{3,5,4,2,1,0:T(8,128)S(1)}) fusion(pred[4,4,128]{2,1,0:T(4,128)(4,1)S(1)} %broadcast_compare_fusion, bf16[4,4,1,8,128,128]{5,4,3,2,1,0:T(8,128)(2,1)} %get-tuple-element.11, bf16[4,3,64,128]{3,2,1,0:T(8,128)(2,1)S(1)} %all-to-all-done.3), kind=kOutput, calls=%fused_computation.20 | convolution fusion | flops 101839872 | bytes 5978112 | tf_op jit(solution)/shard_map/rskgd,rbktd->rskgbt/dot_general | solution.py:84
  161.5 1.2 convert_reduce_fusion.1
  164.2 3.5 %fusion.6 = bf16[4,3,8,8,128]{4,3,1,2,0:T(8,128)(2,1)S(1)} fusion(bf16[4,4,1,8,128,128]{5,4,3,2,1,0:T(8,128)(2,1)} %get-tuple-element.12, f32[4,3,8,8,4]{3,1,4,2,0:T(4,128)S(1)} %get-tuple-element.10, f32[4,8,4,128,3,8]{3,5,4,2,1,0:T(8,128)S(1)} %get-tuple-element.29, f32[4,3,8,8,4]{3,1,4,2,0:T(4,128)S(1)} %get-tuple-element.28, ...), kind=kOutput, calls=%fused_computation.13 | convolution fusion | flops 102531072 | bytes 5990400 | tf_op jit(solution)/shard_map/rskgbt,rbktd->rskgbd/dot_general | solution.py:95
  167.8 1.1 pad_maximum_fusion
  168.9 3.5 %all-to-all-start.4 = ((bf16[4,3,8,8,130]{4,3,2,1,0:T(8,128)(2,1)}), bf16[4,3,8,8,130]{4,3,2,1,0:T(8,128)(2,1)S(1)}, u32[]{:S(2)}, u32[]{:S(2)}) async-start(bf16[4,3,8,8,130]{4,3,2,1,0:T(8,128)(2,1)} %pad_maximum_fusion), calls=%async_computation.4 | async-start | bytes 786432 | tf_op jit(solution)/shard_map/all_to_all | solution.py:48
  172.3 0.8 select_reduce_fusion
  173.4 6.3 %all-to-all-done.4 = bf16[4,3,8,8,130]{4,3,2,1,0:T(8,128)(2,1)S(1)} async-done(((bf16[4,3,8,8,130]{4,3,2,1,0:T(8,128)(2,1)}), bf16[4,3,8,8,130]{4,3,2,1,0:T(8,128)(2,1)S(1)}, u32[]{:S(2)}, u32[]{:S(2)}) %all-to-all-start.4) | async-done | bytes 199712 | tf_op jit(solution)/shard_map/all_to_all | solution.py:48
  181.9 6.5 %copy.286 = bf16[4,3,8,8,128]{0,1,4,3,2:T(4,128)(2,1)} copy(bf16[4,3,8,8,128]{4,3,1,2,0:T(8,128)(2,1)S(1)} %fusion.21) | data formatting | bytes 393216 | tf_op jit(solution)/shard_map/convert_element_type | solution.py:129
  188.4 12.6 %reshape.315 = bf16[32,2,1536]{2,1,0:T(2,128)(2,1)S(1)} reshape(bf16[8192,3,4]{2,1,0:T(4,128)(2,1)} %bitcast.153) | data formatting | bytes 393216
  201.0 14.2 %all_to_all.62 = bf16[32,2,1536]{2,1,0:T(2,128)(2,1)S(1)} all-to-all(bf16[32,2,1536]{2,1,0:T(2,128)(2,1)S(1)} %reshape.315), channel_id=1, replica_groups=mesh['group_0'=2,'group_1'=2,'tensor'=32] {'tensor'}, dimensions={0} | all-to-all | bytes 393216 | tf_op jit(solution)/shard_map/all_to_all | solution.py:210
  215.1 10.4 %reshape.316 = bf16[8192,3,4]{2,1,0:T(4,128)(2,1)} reshape(bf16[32,2,1536]{2,1,0:T(2,128)(2,1)S(1)} %all_to_all.62) | data formatting | bytes 393216
  225.5 7.9 %copy.287 = bf16[4,3,32,256]{3,2,0,1:T(8,128)(2,1)S(1)} copy(bf16[4,3,32,256]{0,1,3,2:T(4,128)(2,1)} %bitcast.154) | data formatting | bytes 393216 | tf_op jit(solution)/shard_map/all_to_all | solution.py:210
  233.6 6.7 %convolution_convert_fusion = bf16[128,3,8192]{2,0,1:T(8,128)(2,1)} fusion(bf16[128,3,256]{2,0,1:T(8,128)(2,1)S(1)} %all_to_all.52, bf16[256,8192]{1,0:T(8,128)(2,1)} %param.11), kind=kOutput, calls=%fused_computation.3 | convolution fusion | flops 1613758464 | bytes 10682368 | tf_op jit(solution)/shard_map/rsc,cd->rsd/dot_general | solution.py:212
  240.3 10.2 %reshape.286 = bf16[32,4,3,8192]{3,1,0,2:T(4,128)(2,1)} reshape(bf16[128,3,8192]{2,0,1:T(8,128)(2,1)} %convolution_convert_fusion) | data formatting | bytes 12582912 | tf_op jit(solution)/shard_map/reshape | solution.py:21
  250.4 5.7 %copy.267 = bf16[32,4,3,8192]{3,1,2,0:T(4,128)(2,1)S(1)} copy(bf16[32,4,3,8192]{3,1,0,2:T(4,128)(2,1)} %reshape.286) | data formatting | bytes 12582912 | tf_op jit(solution)/shard_map/reshape | solution.py:21
  256.1 77.5 %all_to_all.63 = bf16[32,4,3,8192]{3,1,2,0:T(4,128)(2,1)S(1)} all-to-all(bf16[32,4,3,8192]{3,1,2,0:T(4,128)(2,1)S(1)} %copy.267), channel_id=1, replica_groups=mesh['group_0'=2,'group_1'=2,'tensor'=32] {'tensor'}, dimensions={0} | all-to-all | bytes 12582912 | tf_op jit(solution)/shard_map/all_to_all | solution.py:61
  333.6 3.0 convert_reduce_fusion
  336.6 0.8 fusion.26
  (66 shorter events, 12.1 us)
Async XLA Ops:
  6.5 10.9 %copy-start = (s32[1,12]{1,0:T(1,128)S(1)}, s32[1,12]{1,0:T(1,128)}, u32[]{:S(2)}) copy-start(s32[1,12]{1,0:T(1,128)} %param.14) | copy-start | bytes 148
  6.5 110.4 %all-gather.2.cloned.1.call-start = ((), (), s32[]{:S(2)}) async-start(), calls=%async_computation.7 | async-start | bytes 8650752 | tf_op jit(solution)/shard_map/all_gather | solution.py:167
  14.1 18.1 %all-to-all-start.1 = ((s32[2,2,1]{1,2,0:T(1,128)}), s32[2,2,1]{1,2,0:T(1,128)S(1)}, u32[]{:S(2)}, u32[]{:S(2)}) async-start(s32[2,2,1]{1,2,0:T(1,128)} %bitcast.15), calls=%async_computation.1 | async-start | bytes 2048 | tf_op jit(solution)/shard_map/all_to_all | solution.py:35
  130.2 17.1 %all-to-all-start = ((bf16[128,3,320]{2,1,0:T(4,128)(2,1)}), bf16[128,3,320]{2,1,0:T(4,128)(2,1)S(1)}, u32[]{:S(2)}, u32[]{:S(2)}) async-start(bf16[128,3,320]{2,1,0:T(4,128)(2,1)} %copy.229), calls=%async_computation | async-start | bytes 786432 | tf_op jit(solution)/shard_map/all_to_all | solution.py:168
  149.3 8.7 %all-to-all-start.3 = ((bf16[4,3,64,128]{3,2,1,0:T(8,128)(2,1)}), bf16[4,3,64,128]{3,2,1,0:T(8,128)(2,1)S(1)}, u32[]{:S(2)}, u32[]{:S(2)}) async-start(bf16[4,3,64,128]{3,2,1,0:T(8,128)(2,1)} %copy.237), calls=%async_computation.3 | async-start | bytes 393216 | tf_op jit(solution)/shard_map/all_to_all | solution.py:187
  168.9 10.9 %all-to-all-start.4 = ((bf16[4,3,8,8,130]{4,3,2,1,0:T(8,128)(2,1)}), bf16[4,3,8,8,130]{4,3,2,1,0:T(8,128)(2,1)S(1)}, u32[]{:S(2)}, u32[]{:S(2)}) async-start(bf16[4,3,8,8,130]{4,3,2,1,0:T(8,128)(2,1)} %pad_maximum_fusion), calls=%async_computation.4 | async-start | bytes 786432 | tf_op jit(solution)/shard_map/all_to_all | solution.py:48
  256.1 81.3 %copy-start.1 = (s32[1,12]{1,0:T(1,128)S(1)}, s32[1,12]{1,0:T(1,128)}, u32[]{:S(2)}) copy-start(s32[1,12]{1,0:T(1,128)} %param.14) | copy-start | bytes 148
  333.6 3.0 copy-start.2
Sparse Core Ops, SparseCore 0:
  10.5 106.3 all-gather.1
where the time goes:
time: 346 us; the launch traced here: 344 us
  waiting for transfers between devices  103 us (30%)
  blocking collectives  95.3 us (28%)
  local copies, waits for them, and re-layouts  75.1 us (22%)
  matrix products  27.6 us (8%)
  starting transfers between devices  16 us (5%)
  between operations  13.7 us (4%)
  other arithmetic  13.5 us (4%)
    all_gather x1, waiting for transfers between devices, per_device(): lax.all_gather(normed, 'tensor', axis=0, tiled=True)  80.8 us
    all_to_all x1, blocking collectives, summed_on_arrival(): lax.all_to_all(parts, axis, split_axis=0, concat_axis=0, tiled=True)  77.5 us
    unnamed x10, local copies, waits for them, and re-layouts  24.2 us
    reshape x2, local copies, waits for them, and re-layouts, cut_along(): shard.reshape(*lengths[:dim], devices, lengths[dim] // devices, *lengths[...  15.8 us
    all_to_all x1, blocking collectives, per_device(): lax.all_to_all(attended, 'tensor', split_axis=2, concat_axis=0, tiled=True)  14.2 us
    dot_general x1, matrix products, columns(): jnp.einsum('rsd,dc->rsc', row_piece, w_qkv, preferred_element_type=jnp.fl...  12.4 us
    all_to_all x1, waiting for transfers between devices, per_device(): lax.all_to_all(gathered, 'tensor', split_axis=0, concat_axis=2, tiled=True)  11 us
    gather x3, local copies, waits for them, and re-layouts, per_device(): home_pages = page_pool[pool_order[page_slots]]  8.41 us
  transfers between devices with their start and end apart: 5, of which 4 were waited for; matrix products, arithmetic and copies ran while one was open for 6% of the time, Pallas kernels for 0%

commit v1 on v0

--- a/solution.py
+++ b/solution.py
@@ -14,6 +14,11 @@
 EPS = 1e-05
 ROPE_BASE = 500000.0
 NEG_FILL = -1e30
+
+
+def exchange_gather(block, name, along):
+    sent = jnp.stack([block] * lax.axis_size(name))
+    return jnp.concatenate(lax.all_to_all(sent, name, 0, 0), axis=along)
 
 
 def cut_along(shard, dim, devices):
@@ -164,7 +169,7 @@
             "rsd,dc->rsc", row_piece, w_qkv, preferred_element_type=jnp.float32
         ).astype(jnp.bfloat16)
 
-    gathered = columns(lax.all_gather(normed, "tensor", axis=0, tiled=True), jnp.int32(0))
+    gathered = columns(exchange_gather(normed, "tensor", 0), jnp.int32(0))
     full_rows = lax.all_to_all(gathered, "tensor", split_axis=0, concat_axis=2, tiled=True)
     positions = new_lens[:, None] + 0 + jnp.arange(steps_here, dtype=jnp.int32)[None, :]
     queries = rotate(

time: 346 us -> 361 us (1.043)
  local copies, waits for them, and re-layouts: 75.1 us -> 100 us
  between operations: 13.7 us -> 0.29 us
  starting transfers between devices: 16 us -> 27.6 us
  matrix products: 27.6 us -> 22.4 us
    all_gather x1 -> x0, waiting for transfers between devices: 80.8 us -> none  [per_device(): lax.all_gather(normed, 'tensor', axis=0, tiled=True)]
    all_to_all x0 -> x1, waiting for transfers between devices: none -> 75.5 us  [exchange_gather(): return jnp.concatenate(lax.all_to_all(sent, name, 0, 0), axis=along)]
    all_to_all x0 -> x1, starting transfers between devices: none -> 11 us  [exchange_gather(): return jnp.concatenate(lax.all_to_all(sent, name, 0, 0), axis=along)]
    all_to_all x0 -> x1, local copies, waits for them, and re-layouts: none -> 10.7 us  [exchange_gather(): return jnp.concatenate(lax.all_to_all(sent, name, 0, 0), axis=along)]
    reshape x0 -> x1, local copies, waits for them, and re-layouts: none -> 9.72 us  [exchange_gather(): return jnp.concatenate(lax.all_to_all(sent, name, 0, 0), axis=along)]
    another operation x0 -> x1, local copies, waits for them, and re-layouts: none -> 5.66 us  [exchange_gather(): sent = jnp.stack([block] * lax.axis_size(name))]
    dot_general x1, matrix products: 12.4 us -> 7.19 us  [columns(): jnp.einsum('rsd,dc->rsc', row_piece, w_qkv, preferred_element_type=jnp.fl...]
  transfers between devices with their start and end apart: 5 -> 5, of which waited for: 4 -> 5; matrix products, arithmetic and copies ran while one was open for 6% -> 5% of each run, Pallas kernels for 0% -> 0%
where the time goes in v1:
time: 361 us; the launch traced here: 359 us
  local copies, waits for them, and re-layouts  100 us (28%)
  waiting for transfers between devices  99.6 us (28%)
  blocking collectives  95.7 us (27%)
  starting transfers between devices  27.6 us (8%)
  matrix products  22.4 us (6%)
  other arithmetic  13.5 us (4%)
    all_to_all x1, blocking collectives, summed_on_arrival(): lax.all_to_all(parts, axis, split_axis=0, concat_axis=0, tiled=True)  77.5 us
    all_to_all x1, waiting for transfers between devices, exchange_gather(): return jnp.concatenate(lax.all_to_all(sent, name, 0, 0), axis=along)  75.5 us
    unnamed x10, local copies, waits for them, and re-layouts  24.2 us
    reshape x2, local copies, waits for them, and re-layouts, cut_along(): shard.reshape(*lengths[:dim], devices, lengths[dim] // devices, *lengths[...  15.8 us
    all_to_all x1, blocking collectives, per_device(): lax.all_to_all(attended, 'tensor', split_axis=2, concat_axis=0, tiled=True)  14.6 us
    all_to_all x1, waiting for transfers between devices, per_device(): lax.all_to_all(gathered, 'tensor', split_axis=0, concat_axis=2, tiled=True)  11.3 us
    all_to_all x1, starting transfers between devices, exchange_gather(): return jnp.concatenate(lax.all_to_all(sent, name, 0, 0), axis=along)  11 us
    all_to_all x1, local copies, waits for them, and re-layouts, exchange_gather(): return jnp.concatenate(lax.all_to_all(sent, name, 0, 0), axis=along)  10.7 us
  transfers between devices with their start and end apart: 5, of which 5 were waited for; matrix products, arithmetic and copies ran while one was open for 5% of the time, Pallas kernels for 0%

profile of v1, /device:TPU:0, one launch (start us, length us, event | category | flops | bytes accessed | tf_op | source)
XLA Modules:
  0.0 359.3 jit_solution(10977588115887875432)
XLA Ops:
  4.4 3.2 all-to-all-start.2
  7.6 1.1 fusion.20
  8.8 1.1 fusion.22
  9.9 1.4 all-to-all-done.2
  11.4 3.6 %all_to_all.66 = s32[2,2,1]{0,2,1:T(1,128)S(1)} all-to-all(s32[2,2,1]{0,2,1:T(1,128)S(1)} %copy.187), channel_id=1, replica_groups=mesh['group_0'=2,'group_1'=2,'tensor'=32] {'group_1'}, dimensions={1} | all-to-all | bytes 32 | tf_op jit(solution)/shard_map/all_to_all | solution.py:40
  15.0 5.7 %stack.2 = bf16[32,4,3,8192]{3,1,2,0:T(4,128)(2,1)} broadcast(bf16[4,3,8192]{2,0,1:T(4,128)(2,1)S(1)} %fusion.22), dimensions={1,2,3} | broadcast | bytes 6488064 | tf_op jit(solution)/shard_map/stack | solution.py:20
  20.7 11.0 %all-to-all-start = ((bf16[32,4,3,8192]{3,1,2,0:T(4,128)(2,1)}), bf16[32,4,3,8192]{3,1,2,0:T(4,128)(2,1)}, u32[]{:S(2)}, u32[]{:S(2)}) async-start(bf16[32,4,3,8192]{3,1,2,0:T(4,128)(2,1)} %stack.2), calls=%async_computation | async-start | bytes 12582912 | tf_op jit(solution)/shard_map/all_to_all | solution.py:21
  32.7 7.6 %gather_fusion.1 = bf16[16,2,8,128,128]{4,3,2,1,0:T(8,128)(2,1)} fusion(bf16[12,2,8,128,128]{4,3,2,1,0:T(8,128)(2,1)} %bitcast.158, s32[1024]{0:T(1024)S(1)} %pad_clamp_fusion), kind=kCustom, calls=%fused_computation.1 | custom fusion | bytes 16777280 | tf_op jit(solution)/shard_map/gather | solution.py:155
  40.4 6.1 %fusion.43 = (bf16[4,4,1,8,128,128]{5,4,3,2,1,0:T(8,128)(2,1)}, bf16[4,4,1,8,128,128]{5,4,3,2,1,0:T(8,128)(2,1)}) fusion(bf16[4,4,2,8,128,128]{5,4,3,2,1,0:T(8,128)(2,1)} %bitcast.155), kind=kLoop, calls=%fused_computation.106 | loop fusion | bytes 16777216 | tf_op jit(solution)/shard_map/slice | solution.py:90
  46.7 75.5 %all-to-all-done = bf16[32,4,3,8192]{3,1,2,0:T(4,128)(2,1)} async-done(((bf16[32,4,3,8192]{3,1,2,0:T(4,128)(2,1)}), bf16[32,4,3,8192]{3,1,2,0:T(4,128)(2,1)}, u32[]{:S(2)}, u32[]{:S(2)}) %all-to-all-start) | async-done | bytes 6291488 | tf_op jit(solution)/shard_map/all_to_all | solution.py:21
  122.2 10.7 %copy.182 = bf16[32,4,3,8192]{3,1,0,2:T(4,128)(2,1)} copy(bf16[32,4,3,8192]{3,1,2,0:T(4,128)(2,1)} %all-to-all-done) | data formatting | bytes 12582912 | tf_op jit(solution)/shard_map/all_to_all | solution.py:21
  132.9 9.7 %reshape.289 = bf16[128,3,8192]{2,0,1:T(8,128)(2,1)} reshape(bf16[32,4,3,8192]{3,1,0,2:T(4,128)(2,1)} %copy.182) | data formatting | bytes 12582912 | tf_op jit(solution)/shard_map/reshape | solution.py:21
  142.7 7.2 %fusion.15 = bf16[128,3,320]{0,2,1:T(8,128)(2,1)S(1)} fusion(bf16[128,3,8192]{2,0,1:T(8,128)(2,1)} %reshape.289, bf16[8192,320]{0,1:T(8,128)(2,1)} %param.10), kind=kOutput, calls=%fused_computation.26 | convolution fusion | flops 2013388800 | bytes 11780096 | tf_op jit(solution)/shard_map/rsd,dc->rsc/dot_general | solution.py:168
  150.8 6.4 %all-to-all-start.1 = ((bf16[128,3,320]{2,1,0:T(4,128)(2,1)}), bf16[128,3,320]{2,1,0:T(4,128)(2,1)S(1)}, u32[]{:S(2)}, u32[]{:S(2)}) async-start(bf16[128,3,320]{2,1,0:T(4,128)(2,1)} %copy.183), calls=%async_computation.1 | async-start | bytes 786432 | tf_op jit(solution)/shard_map/all_to_all | solution.py:173
  157.4 11.3 %all-to-all-done.1 = bf16[128,3,320]{2,1,0:T(4,128)(2,1)S(1)} async-done(((bf16[128,3,320]{2,1,0:T(4,128)(2,1)}), bf16[128,3,320]{2,1,0:T(4,128)(2,1)S(1)}, u32[]{:S(2)}, u32[]{:S(2)}) %all-to-all-start.1) | async-done | bytes 245792 | tf_op jit(solution)/shard_map/all_to_all | solution.py:173
  170.7 3.5 all-to-all-start.4
  174.4 5.0 %all-to-all-done.4 = bf16[4,3,64,128]{3,2,1,0:T(8,128)(2,1)S(1)} async-done(((bf16[4,3,64,128]{3,2,1,0:T(8,128)(2,1)}), bf16[4,3,64,128]{3,2,1,0:T(8,128)(2,1)S(1)}, u32[]{:S(2)}, u32[]{:S(2)}) %all-to-all-start.4) | async-done | bytes 196640 | tf_op jit(solution)/shard_map/all_to_all | solution.py:192
  179.4 3.6 fusion.9
  183.0 1.2 convert_reduce_fusion.1
  185.7 3.5 fusion.5
  190.3 3.5 all-to-all-start.5
  194.8 6.3 %all-to-all-done.5 = bf16[4,3,8,8,130]{4,3,2,1,0:T(8,128)(2,1)S(1)} async-done(((bf16[4,3,8,8,130]{4,3,2,1,0:T(8,128)(2,1)}), bf16[4,3,8,8,130]{4,3,2,1,0:T(8,128)(2,1)S(1)}, u32[]{:S(2)}, u32[]{:S(2)}) %all-to-all-start.5) | async-done | bytes 199712 | tf_op jit(solution)/shard_map/all_to_all | solution.py:53
  203.3 6.5 %copy.240 = bf16[4,3,8,8,128]{0,1,4,3,2:T(4,128)(2,1)} copy(bf16[4,3,8,8,128]{4,3,1,2,0:T(8,128)(2,1)S(1)} %fusion.18) | data formatting | bytes 393216 | tf_op jit(solution)/shard_map/convert_element_type | solution.py:134
  209.8 12.6 %reshape.321 = bf16[32,2,1536]{2,1,0:T(2,128)(2,1)S(1)} reshape(bf16[8192,3,4]{2,1,0:T(4,128)(2,1)} %bitcast.156) | data formatting | bytes 393216
  222.4 14.6 %all_to_all.67 = bf16[32,2,1536]{2,1,0:T(2,128)(2,1)S(1)} all-to-all(bf16[32,2,1536]{2,1,0:T(2,128)(2,1)S(1)} %reshape.321), channel_id=1, replica_groups=mesh['group_0'=2,'group_1'=2,'tensor'=32] {'tensor'}, dimensions={0} | all-to-all | bytes 393216 | tf_op jit(solution)/shard_map/all_to_all | solution.py:215
  236.9 10.4 %reshape.322 = bf16[8192,3,4]{2,1,0:T(4,128)(2,1)} reshape(bf16[32,2,1536]{2,1,0:T(2,128)(2,1)S(1)} %all_to_all.67) | data formatting | bytes 393216
  247.3 7.9 %copy.241 = bf16[4,3,32,256]{3,2,0,1:T(8,128)(2,1)S(1)} copy(bf16[4,3,32,256]{0,1,3,2:T(4,128)(2,1)} %bitcast.157) | data formatting | bytes 393216 | tf_op jit(solution)/shard_map/all_to_all | solution.py:215
  255.4 6.7 %convolution_convert_fusion = bf16[128,3,8192]{2,0,1:T(8,128)(2,1)} fusion(bf16[128,3,256]{2,0,1:T(8,128)(2,1)S(1)} %all_to_all.56, bf16[256,8192]{1,0:T(8,128)(2,1)} %param.11), kind=kOutput, calls=%fused_computation.3 | convolution fusion | flops 1613758464 | bytes 10682368 | tf_op jit(solution)/shard_map/rsc,cd->rsd/dot_general | solution.py:217
  262.1 10.2 %reshape.292 = bf16[32,4,3,8192]{3,1,0,2:T(4,128)(2,1)} reshape(bf16[128,3,8192]{2,0,1:T(8,128)(2,1)} %convolution_convert_fusion) | data formatting | bytes 12582912 | tf_op jit(solution)/shard_map/reshape | solution.py:26
  272.3 5.7 %copy.221 = bf16[32,4,3,8192]{3,1,2,0:T(4,128)(2,1)S(1)} copy(bf16[32,4,3,8192]{3,1,0,2:T(4,128)(2,1)} %reshape.292) | data formatting | bytes 12582912 | tf_op jit(solution)/shard_map/reshape | solution.py:26
  277.9 77.5 %all_to_all.68 = bf16[32,4,3,8192]{3,1,2,0:T(4,128)(2,1)S(1)} all-to-all(bf16[32,4,3,8192]{3,1,2,0:T(4,128)(2,1)S(1)} %copy.221), channel_id=1, replica_groups=mesh['group_0'=2,'group_1'=2,'tensor'=32] {'tensor'}, dimensions={0} | all-to-all | bytes 12582912 | tf_op jit(solution)/shard_map/all_to_all | solution.py:66
  355.4 3.0 convert_reduce_fusion
  (67 shorter events, 15.7 us)
Async XLA Ops:
  0.0 31.8 %copy-start = (s32[1,12]{1,0:T(1,128)S(1)}, s32[1,12]{1,0:T(1,128)}, u32[]{:S(2)}) copy-start(s32[1,12]{1,0:T(1,128)} %param.14) | copy-start | bytes 148
  4.4 6.9 %all-to-all-start.2 = ((s32[2,2,1]{1,2,0:T(1,128)}), s32[2,2,1]{1,2,0:T(1,128)S(1)}, u32[]{:S(2)}, u32[]{:S(2)}) async-start(s32[2,2,1]{1,2,0:T(1,128)} %bitcast.15), calls=%async_computation.2 | async-start | bytes 2048 | tf_op jit(solution)/shard_map/all_to_all | solution.py:40
  20.7 101.5 %all-to-all-start = ((bf16[32,4,3,8192]{3,1,2,0:T(4,128)(2,1)}), bf16[32,4,3,8192]{3,1,2,0:T(4,128)(2,1)}, u32[]{:S(2)}, u32[]{:S(2)}) async-start(bf16[32,4,3,8192]{3,1,2,0:T(4,128)(2,1)} %stack.2), calls=%async_computation | async-start | bytes 12582912 | tf_op jit(solution)/shard_map/all_to_all | solution.py:21
  150.8 18.0 %all-to-all-start.1 = ((bf16[128,3,320]{2,1,0:T(4,128)(2,1)}), bf16[128,3,320]{2,1,0:T(4,128)(2,1)S(1)}, u32[]{:S(2)}, u32[]{:S(2)}) async-start(bf16[128,3,320]{2,1,0:T(4,128)(2,1)} %copy.183), calls=%async_computation.1 | async-start | bytes 786432 | tf_op jit(solution)/shard_map/all_to_all | solution.py:173
  170.7 8.7 %all-to-all-start.4 = ((bf16[4,3,64,128]{3,2,1,0:T(8,128)(2,1)}), bf16[4,3,64,128]{3,2,1,0:T(8,128)(2,1)S(1)}, u32[]{:S(2)}, u32[]{:S(2)}) async-start(bf16[4,3,64,128]{3,2,1,0:T(8,128)(2,1)} %copy.191), calls=%async_computation.4 | async-start | bytes 393216 | tf_op jit(solution)/shard_map/all_to_all | solution.py:192
  190.3 10.9 %all-to-all-start.5 = ((bf16[4,3,8,8,130]{4,3,2,1,0:T(8,128)(2,1)}), bf16[4,3,8,8,130]{4,3,2,1,0:T(8,128)(2,1)S(1)}, u32[]{:S(2)}, u32[]{:S(2)}) async-start(bf16[4,3,8,8,130]{4,3,2,1,0:T(8,128)(2,1)} %pad_maximum_fusion), calls=%async_computation.5 | async-start | bytes 786432 | tf_op jit(solution)/shard_map/all_to_all | solution.py:53
  277.9 81.3 %copy-start.1 = (s32[1,12]{1,0:T(1,128)S(1)}, s32[1,12]{1,0:T(1,128)}, u32[]{:S(2)}) copy-start(s32[1,12]{1,0:T(1,128)} %param.14) | copy-start | bytes 148
  355.4 3.0 copy-start.2
